TPU v7x, 32 devices: a whole 2x2x4 slice. The times are simulated.
32 devices in a mesh: groups: 2 (over y), wide: 4 (over z), dp: 2 (over x), expert: 2 (over core).
Axes of the slice: x: 2, y: 2, z: 4, core: 2. Of those that a mesh axis runs over, the one named last changes fastest.
Arguments:
- tokens: bfloat16 [2, 2048, 4096], P('expert', ('groups', 'wide', 'dp')), parts along dimension 1, may hold values from -6 to 6
- cotangent: bfloat16 [2, 2048, 1536], P('expert', ('groups', 'wide', 'dp')), parts along dimension 1, may hold values from -6 to 6
- frozen_up_weight: bfloat16 [2, 4096, 1536], P('expert', None, 'dp'), may hold values from -0.09375 to 0.09375
- master: float32 [4, 32, 5632], P(('groups', 'expert'), None, ('wide', 'dp')), parts along dimension 0, may hold values from -0.3 to 0.3
- moment_one: float32 [4, 32, 5632], P(('groups', 'expert'), None, ('wide', 'dp')), parts along dimension 0, may hold values from -0.12 to 0.12
- moment_two: float32 [4, 32, 5632], P(('groups', 'expert'), None, ('wide', 'dp')), parts along dimension 0, may hold values from 0.0001 to 0.001
Outputs:
- merged: bfloat16 [4, 4096, 1536], P(('groups', 'expert'), None, 'dp'), parts along dimension 0
- renewed: float32 [4, 32, 5632], P(('groups', 'expert'), None, ('wide', 'dp')), parts along dimension 0
There are 2 independent parts, one for each index of `groups`. A program takes and returns all parts, laid end to end along the dimension named above; an argument that names none is the same for every part. Nothing has to cross between parts.
All inputs are finite; a program needn't handle non-finite values.
Results may differ from a plain program's by a relative error of at most 0.0056.
Values may be sent and summed in bfloat16 or wider, within the bound.
A program may use at most 64 MiB of HBM per device.

v0:
```python
import jax
import jax.numpy as jnp
from jax import lax
from jax.sharding import PartitionSpec as P

beta_one = 0.9
beta_two = 0.95
learn_rate = 0.01
weight_decay = 0.1
step_count = 10
eps_adam = 1e-08
low_rank_scale = 2.0


def shards(tokens, cotangent, frozen_up_weight, master, moment_one, moment_two):
    wide_count = lax.axis_size("wide")
    data_count = lax.axis_size("dp")
    width = tokens.shape[2]
    inputs = tokens[0]
    upstream = cotangent[0]
    current = master[0].astype(jnp.bfloat16)
    gathered = lax.all_gather(current, ("wide", "dp"), axis=1, tiled=True)
    rows_b = gathered[:, :width]
    cols_a = gathered[:, width:]
    hidden = jnp.dot(inputs, rows_b.T, preferred_element_type=jnp.float32).astype(jnp.bfloat16)
    back = jnp.dot(upstream, cols_a.T, preferred_element_type=jnp.float32).astype(jnp.bfloat16)
    up_factor = jnp.dot(back.T, inputs, preferred_element_type=jnp.float32)
    down_factor = jnp.dot(hidden.T, upstream, preferred_element_type=jnp.float32)
    partial_value = jnp.concatenate([up_factor, down_factor], axis=1)
    reduced_total = lax.psum_scatter(partial_value, ("wide", "dp"), scatter_dimension=1, tiled=True)
    gathered_rows = inputs.shape[0] * wide_count * data_count
    adapter_gradient = reduced_total * (low_rank_scale / gathered_rows)
    first_new = beta_one * moment_one[0] + (1.0 - beta_one) * adapter_gradient
    second_new = beta_two * moment_two[0] + (1.0 - beta_two) * adapter_gradient * adapter_gradient
    step_size = (
        first_new
        / (1.0 - beta_one**step_count)
        / (jnp.sqrt(second_new / (1.0 - beta_two**step_count)) + eps_adam)
    )
    renewed = master[0] - learn_rate * (step_size + weight_decay * master[0])
    factors = renewed.astype(jnp.bfloat16)
    all_factors = lax.all_gather(factors, ("wide", "dp"), axis=1, tiled=True)
    slice_width = frozen_up_weight.shape[2]
    data_index = lax.axis_index("dp")
    new_b = all_factors[:, :width]
    new_a = lax.dynamic_slice_in_dim(all_factors, width + data_index * slice_width, slice_width, 1)
    factor_product = jnp.dot(new_b.T, new_a, preferred_element_type=jnp.float32)
    merged = (frozen_up_weight[0].astype(jnp.float32) + low_rank_scale * factor_product).astype(
        jnp.bfloat16
    )
    return (merged[None], renewed[None])


def solution(mesh):
    in_specs = (
        P("expert", ("groups", "wide", "dp"), None),
        P("expert", ("groups", "wide", "dp"), None),
        P("expert", None, "dp"),
        P(("groups", "expert"), None, ("wide", "dp")),
        P(("groups", "expert"), None, ("wide", "dp")),
        P(("groups", "expert"), None, ("wide", "dp")),
    )
    out_specs = (P(("groups", "expert"), None, "dp"), P(("groups", "expert"), None, ("wide", "dp")))
    return jax.shard_map(shards, mesh=mesh, in_specs=in_specs, out_specs=out_specs, check_vma=False)
```

profile of v0, /device:TPU:0, one launch (start us, length us, event | category | flops | bytes accessed | tf_op | source)
XLA Modules:
  0.0 167.9 jit_solution(12773097675333313434)
XLA Ops:
  7.2 0.0 copy-start
  7.2 0.0 reduce-scatter.4.cloned.1.call-start
  7.2 1.0 fusion.23
  8.2 32.7 %all-gather = bf16[8,704,32]{1,2,0:T(8,128)(2,1)S(1)} all-gather(bf16[1,704,32]{1,2,0:T(8,128)(2,1)S(1)} %fusion.23), channel_id=1, replica_groups=mesh['groups'=2,'wide'=4,'dp'=2,'expert'=2] {'wide','dp'}, dimensions={0}, use_global_device_ids=true | all-gather | bytes 405504 | tf_op jit(solution)/shard_map/all_gather | solution.py:22
  40.9 0.2 copy.10
  41.2 0.3 reshape.12
  41.5 0.0 copy-start.1
  41.5 0.0 copy-start.2
  41.5 0.0 copy-start.3
  41.5 0.0 copy-done
  41.6 1.8 %fusion.3 = f32[32,1536]{1,0:T(8,128)S(1)} fusion(bf16[1,128,4096]{2,1,0:T(8,128)(2,1)S(1)} %copy-done, bf16[1,128,1536]{2,1,0:T(8,128)(2,1)} %param.7, bf16[32,5632]{1,0:T(8,128)(2,1)S(1)} %bitcast.70), kind=kOutput, calls=%fused_computation.6 | convolution fusion | flops 46141440 | bytes 1900544 | tf_op jit(solution)/shard_map/dot_general | solution.py:28
  43.3 1.7 fusion.2
  45.0 0.1 pad_maximum_fusion
  45.0 2.1 %copy.12 = f32[32,5632]{0,1:T(8,128)} copy(f32[32,5632]{1,0:T(8,128)S(1)} %pad_maximum_fusion) | data formatting | bytes 1441792
  47.1 0.0 reduce-scatter.4.cloned.1.call-update
  47.2 73.0 %reduce-scatter.4.cloned.1.call-done = f32[704,32]{1,0:T(8,128)} async-done(((f32[5632,32]{1,0:T(8,128)}), f32[704,32]{1,0:T(8,128)}) %reduce-scatter.4.cloned.1.call-update) | async-done | bytes 90128
  120.2 1.1 copy.13
  121.3 0.0 copy-done.1
  121.3 0.0 copy-done.2
  121.3 0.0 copy-done.3
  121.3 0.7 convert_bitcast_fusion
  122.1 31.1 %all-gather.1 = bf16[8,704,32]{1,2,0:T(8,128)(2,1)S(1)} all-gather(bf16[1,704,32]{1,2,0:T(8,128)(2,1)S(1)} %get-tuple-element.2), channel_id=1, replica_groups=mesh['groups'=2,'wide'=4,'dp'=2,'expert'=2] {'wide','dp'}, dimensions={0}, use_global_device_ids=true | all-gather | bytes 405504 | tf_op jit(solution)/shard_map/all_gather | solution.py:42
  153.1 0.2 copy.11
  153.4 0.3 reshape.14
  153.7 7.3 %fusion.1 = bf16[1,4096,768]{2,1,0:T(8,128)(2,1)} fusion(bf16[1,4096,768]{2,1,0:T(8,128)(2,1)} %param.8, bf16[32,5632]{1,0:T(8,128)(2,1)S(1)} %bitcast.72, bf16[5632,32]{0,1:T(8,128)(2,1)S(1)} %reshape.14, s32[]{:T(128)S(6)} %select_n.3), kind=kOutput, calls=%fused_computation.2 | convolution fusion | flops 213909504 | bytes 12894212 | tf_op jit(solution)/shard_map/dot_general | solution.py:47
Async XLA Ops:
  7.2 34.4 %copy-start = (bf16[1,128,4096]{2,1,0:T(8,128)(2,1)S(1)}, bf16[1,128,4096]{2,1,0:T(8,128)(2,1)}, u32[]{:S(2)}) copy-start(bf16[1,128,4096]{2,1,0:T(8,128)(2,1)} %param.6) | copy-start | bytes 3145732
  7.2 113.0 %reduce-scatter.4.cloned.1.call-start = ((), (), s32[]{:S(2)}) async-start(), calls=%async_computation.1 | async-start | bytes 3244032
  41.5 79.8 %copy-start.1 = (f32[1,32,704]{2,1,0:T(8,128)S(1)}, f32[1,32,704]{2,1,0:T(8,128)}, u32[]{:S(2)}) copy-start(f32[1,32,704]{2,1,0:T(8,128)} %param.9) | copy-start | bytes 270340
  41.5 79.8 %copy-start.2 = (f32[1,32,704]{2,1,0:T(8,128)S(1)}, f32[1,32,704]{2,1,0:T(8,128)}, u32[]{:S(2)}) copy-start(f32[1,32,704]{2,1,0:T(8,128)} %param.11) | copy-start | bytes 270340
  41.5 79.8 %copy-start.3 = (f32[1,32,704]{2,1,0:T(8,128)S(1)}, f32[1,32,704]{2,1,0:T(8,128)}, u32[]{:S(2)}) copy-start(f32[1,32,704]{2,1,0:T(8,128)} %param.10) | copy-start | bytes 270340
Sparse Core Ops, SparseCore 0:
  47.3 72.8 reduce-scatter.3
where the time goes:
time: 168 us
  waiting for transfers between devices  73 us (43%)
  blocking collectives  63.8 us (38%)
  between operations  14.1 us (8%)
  matrix products  10.8 us (6%)
  local copies, waits for them, and re-layouts  4.34 us (3%)
  other arithmetic  1.77 us (1%)
    unnamed x2, waiting for transfers between devices  73 us
    all_gather x1, blocking collectives, shards(): gathered = lax.all_gather(current, ('wide', 'dp'), axis=1, tiled=True)  32.7 us
    all_gather x1, blocking collectives, shards(): all_factors = lax.all_gather(factors, ('wide', 'dp'), axis=1, tiled=True)  31.1 us
    dot_general x1, matrix products, shards(): factor_product = jnp.dot(new_b.T, new_a, preferred_element_type=jnp.float32)  7.34 us
    unnamed x12, local copies, waits for them, and re-layouts  3.9 us
  transfers between devices with their start and end apart: 1, of which 1 were waited for; matrix products, arithmetic and copies ran while one was open for 0% of the time, Pallas kernels for 0%

commit v1 on v0

--- a/solution.py
+++ b/solution.py
@@ -1,6 +1,10 @@
+import functools
+
 import jax
 import jax.numpy as jnp
 from jax import lax
+from jax.experimental import pallas as pl
+from jax.experimental.pallas import tpu as pltpu
 from jax.sharding import PartitionSpec as P
 
 beta_one = 0.9
@@ -10,6 +14,273 @@
 step_count = 10
 eps_adam = 1e-08
 low_rank_scale = 2.0
+
+MESH = pl.DeviceIdType.MESH
+NT = (((1,), (1,)), ((), ()))
+TN = (((0,), (0,)), ((), ()))
+
+
+def adam(master, moment_one, moment_two, gradient):
+    first_new = beta_one * moment_one + (1.0 - beta_one) * gradient
+    second_new = beta_two * moment_two + (1.0 - beta_two) * gradient * gradient
+    step_size = (
+        first_new
+        / (1.0 - beta_one**step_count)
+        / (jnp.sqrt(second_new / (1.0 - beta_two**step_count)) + eps_adam)
+    )
+    return master - learn_rate * (step_size + weight_decay * master)
+
+
+def update_kernel(
+    nz, scale, tok, cot, mas, mom1, mom2, ren, out_b, out_a,
+    both, frame, gat, fac, snd_x, rcv_x, own, snd_z, rcv_z, allf,
+    in_sem, g_send, g_recv, x_send, x_recv, z_send, z_recv, f_send, f_recv,
+):
+    width = tok.shape[2]
+    hidden_units = cot.shape[2]
+    rank, block = mas.shape[1], mas.shape[2]
+    lanes = gat.shape[3]
+    main = lanes - 128
+    pair = 2 * block
+    shift = lanes - block
+    z = lax.axis_index("wide")
+    x = lax.axis_index("dp")
+    xo = 1 - x
+
+    def z_at(distance):
+        return lax.rem(z + distance, nz)
+
+    in_tok = pltpu.make_async_copy(tok.at[0], both.at[:, pl.ds(0, width)], in_sem.at[0])
+    in_cot = pltpu.make_async_copy(cot.at[0], both.at[:, pl.ds(width, hidden_units)], in_sem.at[1])
+    in_tok.start()
+    in_cot.start()
+
+    barrier = pltpu.get_barrier_semaphore()
+    for d in range(1, nz):
+        pl.semaphore_signal(barrier, inc=1, device_id={"wide": z_at(d)}, device_id_type=MESH)
+    pl.semaphore_signal(barrier, inc=1, device_id={"dp": xo}, device_id_type=MESH)
+
+    def framed(ref):
+        frame[:, main:] = jnp.zeros((rank, 128), jnp.float32)
+        frame[:, :block] = ref[0]
+        return pltpu.roll(frame[...], x * shift, 1)
+
+    master = framed(mas)
+    gat[x, z] = master.astype(jnp.bfloat16)
+    pl.semaphore_wait(barrier, nz)
+
+    def share(buf, send, recv):
+        sends = []
+        for d in range(1, nz):
+            sends.append(pltpu.make_async_remote_copy(
+                buf.at[x, z], buf.at[x, z], send.at[d - 1], recv.at[x, z],
+                device_id={"wide": z_at(d)}, device_id_type=MESH))
+        sends.append(pltpu.make_async_remote_copy(
+            buf.at[x, z], buf.at[x, z], send.at[nz - 1], recv.at[x, z],
+            device_id={"dp": xo}, device_id_type=MESH))
+        for copy in sends:
+            copy.start()
+        return sends
+
+    def arrived(buf, recv, column, row):
+        pltpu.make_async_remote_copy(
+            buf.at[column, row], buf.at[column, row], recv.at[column, row], recv.at[column, row],
+            device_id={"dp": xo}, device_id_type=MESH).wait_recv()
+
+    def forward(buf, send, recv, d):
+        row = z_at(nz - d)
+        arrived(buf, recv, x, row)
+        copy = pltpu.make_async_remote_copy(
+            buf.at[x, row], buf.at[x, row], send.at[nz - 1 + d], recv.at[x, row],
+            device_id={"dp": xo}, device_id_type=MESH)
+        copy.start()
+        return copy
+
+    def start_of(row, column):
+        return row * pair + column * main_step
+
+    main_step = block - shift
+
+    def is_b(row, column):
+        begin = start_of(row, column)
+        return begin < width, begin + main < width
+
+    sends = share(gat, g_send, g_recv)
+    in_tok.wait()
+    in_cot.wait()
+
+    hidden = jnp.zeros((rank, both.shape[0]), jnp.float32)
+    back = jnp.zeros((rank, both.shape[0]), jnp.float32)
+
+    def project(row, column, hidden, back):
+        begin = start_of(row, column)
+        b_main, b_last = is_b(row, column)
+        part = lax.dot_general(
+            gat[column, row, :, :main], both[:, pl.ds(pl.multiple_of(begin, 128), main)],
+            NT, preferred_element_type=jnp.float32)
+        last = lax.dot_general(
+            gat[column, row, :, main:], both[:, pl.ds(pl.multiple_of(begin + main, 128), 128)],
+            NT, preferred_element_type=jnp.float32)
+        hidden = hidden + jnp.where(b_main, part, 0.0) + jnp.where(b_last, last, 0.0)
+        back = back + jnp.where(b_main, 0.0, part) + jnp.where(b_last, 0.0, last)
+        return hidden, back
+
+    for d in range(nz):
+        if d:
+            sends.append(forward(gat, g_send, g_recv, d))
+        hidden, back = project(z_at(nz - d), x, hidden, back)
+    for d in range(nz):
+        row = z_at(nz - d)
+        arrived(gat, g_recv, xo, row)
+        hidden, back = project(row, xo, hidden, back)
+    for copy in sends:
+        copy.wait_send()
+    hidden = hidden.astype(jnp.bfloat16).astype(jnp.float32)
+    back = back.astype(jnp.bfloat16).astype(jnp.float32)
+
+    def gradient(row, column):
+        begin = start_of(row, column)
+        b_main, b_last = is_b(row, column)
+        part = jnp.dot(
+            jnp.where(b_main, back, hidden).astype(jnp.bfloat16),
+            both[:, pl.ds(pl.multiple_of(begin, 128), main)], preferred_element_type=jnp.float32)
+        last = jnp.dot(
+            jnp.where(b_last, back, hidden).astype(jnp.bfloat16),
+            both[:, pl.ds(pl.multiple_of(begin + main, 128), 128)], preferred_element_type=jnp.float32)
+        return part, last
+
+    x_copies = []
+    for i in range(nz):
+        row = z_at(i + 1)
+        part, last = gradient(row, xo)
+        snd_x[row, :, :main] = part.astype(jnp.bfloat16)
+        snd_x[row, :, main:] = last.astype(jnp.bfloat16)
+        copy = pltpu.make_async_remote_copy(
+            snd_x.at[row], rcv_x.at[row], x_send.at[i], x_recv.at[row],
+            device_id={"dp": xo}, device_id_type=MESH)
+        copy.start()
+        x_copies.append(copy)
+    for i in range(nz):
+        row = z_at(i + 1)
+        part, last = gradient(row, x)
+        own[row, :, :main] = part
+        own[row, :, main:] = last
+
+    moment_one = framed(mom1)
+    moment_two = framed(mom2)
+
+    z_copies = []
+    for i in range(nz - 1):
+        row = z_at(i + 1)
+        x_copies[i].wait_recv()
+        snd_z[i] = (own[row] + rcv_x[row].astype(jnp.float32)).astype(jnp.bfloat16)
+        copy = pltpu.make_async_remote_copy(
+            snd_z.at[i], rcv_z.at[z], z_send.at[i], z_recv.at[z],
+            device_id={"wide": row}, device_id_type=MESH)
+        copy.start()
+        z_copies.append(copy)
+    x_copies[nz - 1].wait_recv()
+    total = own[z] + rcv_x[z].astype(jnp.float32)
+    for d in range(1, nz):
+        row = z_at(nz - d)
+        pltpu.make_async_remote_copy(
+            snd_z.at[d - 1], rcv_z.at[row], z_send.at[d - 1], z_recv.at[row],
+            device_id={"wide": row}, device_id_type=MESH).wait_recv()
+        total = total + rcv_z[row].astype(jnp.float32)
+
+    renewed = adam(master, moment_one, moment_two, total * scale)
+    lane = lax.broadcasted_iota(jnp.int32, (rank, lanes), 1)
+    first = x * shift
+    valid = (lane >= first) & (lane < first + block)
+    fac[x, z] = jnp.where(valid, renewed, 0.0).astype(jnp.bfloat16)
+    sends = share(fac, f_send, f_recv)
+    frame[...] = pltpu.roll(renewed, lanes - x * shift, 1)
+    ren[0] = frame[:, :block]
+
+    for copy in x_copies + z_copies:
+        copy.wait_send()
+    for d in range(1, nz):
+        sends.append(forward(fac, f_send, f_recv, d))
+    for d in range(nz):
+        arrived(fac, f_recv, xo, z_at(nz - d))
+    for row in range(nz):
+        base = row * pair
+        allf[:, base:base + main] = fac[0, row, :, :main]
+        joined = fac[0, row, :, main:].astype(jnp.float32) + fac[1, row, :, :128].astype(jnp.float32)
+        allf[:, base + main:base + lanes] = joined.astype(jnp.bfloat16)
+        allf[:, base + lanes:base + pair] = fac[1, row, :, 128:]
+    slice_width = out_a.shape[1]
+    out_b[...] = allf[:, :width]
+    mine = allf[:, pl.ds(pl.multiple_of(width + x * slice_width, 128), slice_width)]
+    out_a[...] = (mine.astype(jnp.float32) * low_rank_scale).astype(jnp.bfloat16)
+    for copy in sends:
+        copy.wait_send()
+
+
+def merge_kernel(weight, new_b, new_a, merged):
+    product = lax.dot_general(new_b[...], new_a[...], TN, preferred_element_type=jnp.float32)
+    merged[0] = (weight[0].astype(jnp.float32) + product).astype(jnp.bfloat16)
+
+
+def fused_shards(nz, tokens, cotangent, frozen_up_weight, master, moment_one, moment_two):
+    rows, width = tokens.shape[1:]
+    hidden_units = cotangent.shape[2]
+    rank, block = master.shape[1:]
+    slice_width = frozen_up_weight.shape[2]
+    lanes = block + 64
+    bf16, f32 = jnp.bfloat16, jnp.float32
+    vmem = pl.BlockSpec(memory_space=pltpu.VMEM)
+    anywhere = pl.BlockSpec(memory_space=pl.ANY)
+    dma = pltpu.SemaphoreType.DMA
+    scale = low_rank_scale / (rows * nz * 2)
+    renewed, new_b, new_a = pl.pallas_call(
+        functools.partial(update_kernel, nz, scale),
+        out_shape=(
+            jax.ShapeDtypeStruct(master.shape, f32),
+            jax.ShapeDtypeStruct((rank, width), bf16),
+            jax.ShapeDtypeStruct((rank, slice_width), bf16),
+        ),
+        in_specs=[anywhere, anywhere, vmem, vmem, vmem],
+        out_specs=(vmem, vmem, vmem),
+        scratch_shapes=[
+            pltpu.VMEM((rows, width + hidden_units), bf16),
+            pltpu.VMEM((rank, lanes), f32),
+            pltpu.VMEM((2, nz, rank, lanes), bf16),
+            pltpu.VMEM((2, nz, rank, lanes), bf16),
+            pltpu.VMEM((nz, rank, lanes), bf16),
+            pltpu.VMEM((nz, rank, lanes), bf16),
+            pltpu.VMEM((nz, rank, lanes), f32),
+            pltpu.VMEM((nz - 1, rank, lanes), bf16),
+            pltpu.VMEM((nz, rank, lanes), bf16),
+            pltpu.VMEM((rank, width + hidden_units), bf16),
+            dma((2,)),
+            dma((2 * nz - 1,)),
+            dma((2, nz)),
+            dma((nz,)),
+            dma((nz,)),
+            dma((nz - 1,)),
+            dma((nz,)),
+            dma((2 * nz - 1,)),
+            dma((2, nz)),
+        ],
+        compiler_params=pltpu.CompilerParams(
+            collective_id=0, has_side_effects=True, vmem_limit_bytes=12 * 1024 * 1024
+        ),
+    )(tokens, cotangent, master, moment_one, moment_two)
+    step = 512
+    merged = pl.pallas_call(
+        merge_kernel,
+        grid=(width // step,),
+        out_shape=jax.ShapeDtypeStruct(frozen_up_weight.shape, bf16),
+        in_specs=[
+            pl.BlockSpec((1, step, slice_width), lambda i: (0, i, 0)),
+            pl.BlockSpec((rank, step), lambda i: (0, i)),
+            pl.BlockSpec((rank, slice_width), lambda i: (0, 0)),
+        ],
+        out_specs=pl.BlockSpec((1, step, slice_width), lambda i: (0, i, 0)),
+        compiler_params=pltpu.CompilerParams(vmem_limit_bytes=16 * 1024 * 1024),
+    )(frozen_up_weight, new_b, new_a)
+    return merged, renewed
 
 
 def shards(tokens, cotangent, frozen_up_weight, master, moment_one, moment_two):
@@ -30,14 +301,7 @@
     reduced_total = lax.psum_scatter(partial_value, ("wide", "dp"), scatter_dimension=1, tiled=True)
     gathered_rows = inputs.shape[0] * wide_count * data_count
     adapter_gradient = reduced_total * (low_rank_scale / gathered_rows)
-    first_new = beta_one * moment_one[0] + (1.0 - beta_one) * adapter_gradient
-    second_new = beta_two * moment_two[0] + (1.0 - beta_two) * adapter_gradient * adapter_gradient
-    step_size = (
-        first_new
-        / (1.0 - beta_one**step_count)
-        / (jnp.sqrt(second_new / (1.0 - beta_two**step_count)) + eps_adam)
-    )
-    renewed = master[0] - learn_rate * (step_size + weight_decay * master[0])
+    renewed = adam(master[0], moment_one[0], moment_two[0], adapter_gradient)
     factors = renewed.astype(jnp.bfloat16)
     all_factors = lax.all_gather(factors, ("wide", "dp"), axis=1, tiled=True)
     slice_width = frozen_up_weight.shape[2]
@@ -51,7 +315,26 @@
     return (merged[None], renewed[None])
 
 
+def frame_fits(nz, nx, width, block, slice_width):
+    if nx != 2 or nz < 2 or nz > 8 or block % 128 != 64 or block < 192 or width % 512 or slice_width % 128:
+        return False
+    for row in range(nz):
+        for column in range(2):
+            begin = row * 2 * block + column * (block - 64)
+            if begin < width < begin + block - 64:
+                return False
+    return True
+
+
 def solution(mesh):
+    nz, nx = mesh.shape["wide"], mesh.shape["dp"]
+
+    def per_device(tokens, cotangent, frozen_up_weight, master, moment_one, moment_two):
+        args = (tokens, cotangent, frozen_up_weight, master, moment_one, moment_two)
+        if frame_fits(nz, nx, tokens.shape[2], master.shape[2], frozen_up_weight.shape[2]):
+            return fused_shards(nz, *args)
+        return shards(*args)
+
     in_specs = (
         P("expert", ("groups", "wide", "dp"), None),
         P("expert", ("groups", "wide", "dp"), None),
@@ -61,4 +344,4 @@
         P(("groups", "expert"), None, ("wide", "dp")),
     )
     out_specs = (P(("groups", "expert"), None, "dp"), P(("groups", "expert"), None, ("wide", "dp")))
-    return jax.shard_map(shards, mesh=mesh, in_specs=in_specs, out_specs=out_specs, check_vma=False)
+    return jax.shard_map(per_device, mesh=mesh, in_specs=in_specs, out_specs=out_specs, check_vma=False)

time: 168 us -> 48.9 us (0.29)
  waiting for transfers between devices: 73 us -> 0 us
  blocking collectives: 63.8 us -> 0 us
  Pallas kernels: 0 us -> 39.6 us
  between operations: 14.1 us -> 0.66 us
  matrix products: 10.8 us -> 0 us
  local copies, waits for them, and re-layouts: 4.34 us -> 8.31 us
  other arithmetic: 1.77 us -> 0 us
    unnamed x2 -> x0, waiting for transfers between devices: 73 us -> none
    all_gather x2 -> x0, blocking collectives: 63.8 us -> none  [the longest x1 32.7 us: shards(): gathered = lax.all_gather(current, ('wide', 'dp'), axis=1, tiled=True)]
    pallas_call x0 -> x2, Pallas kernels: none -> 39.6 us  [the longest x1 34.1 us: fused_shards(): pl.pallas_call(functools.partial(update_kernel, nz, scale), out_shape=(ja...]
    dot_general x3 -> x0, matrix products: 10.8 us -> none  [the longest x1 7.34 us: shards(): factor_product = jnp.dot(new_b.T, new_a, preferred_element_type=jnp.float32)]
    unnamed x12 -> x13, local copies, waits for them, and re-layouts: 3.9 us -> 8.31 us
    unnamed x2 -> x0, other arithmetic: 1.71 us -> none
  transfers between devices with their start and end apart: 1 -> 0, of which waited for: 1 -> 0; matrix products, arithmetic and copies ran while one was open for 0% -> 0% of each run, Pallas kernels for 0% -> 0%
where the time goes in v1:
time: 48.9 us; the launch traced here: 48.6 us
  Pallas kernels  39.6 us (81%)
  local copies, waits for them, and re-layouts  8.31 us (17%)
  between operations  0.66 us (1%)
    pallas_call x1, Pallas kernels, fused_shards(): pl.pallas_call(functools.partial(update_kernel, nz, scale), out_shape=(ja...  34.1 us
    unnamed x13, local copies, waits for them, and re-layouts  8.31 us
    pallas_call x1, Pallas kernels, fused_shards(): pl.pallas_call(merge_kernel, grid=(width // step,), out_shape=jax.ShapeDt...  5.5 us

profile of v1, /device:TPU:0, one launch (start us, length us, event | category | flops | bytes accessed | tf_op | source)
XLA Modules:
  0.0 48.6 jit_solution(16763219517102721754)
XLA Ops:
  0.6 0.0 copy-start.1
  0.6 1.2 %copy-done.1 = bf16[1,128,4096]{2,1,0:T(8,128)(2,1)S(1)} copy-done((bf16[1,128,4096]{2,1,0:T(8,128)(2,1)S(1)}, bf16[1,128,4096]{2,1,0:T(8,128)(2,1)}, u32[]{:S(2)}) %copy-start.1) | copy-done | bytes 1048600
  1.9 0.0 copy-start.2
  1.9 1.0 %copy-done.2 = bf16[1,128,1536]{2,1,0:T(8,128)(2,1)S(1)} copy-done((bf16[1,128,1536]{2,1,0:T(8,128)(2,1)S(1)}, bf16[1,128,1536]{2,1,0:T(8,128)(2,1)}, u32[]{:S(2)}) %copy-start.2) | copy-done | bytes 393240
  2.9 0.0 copy-start.3
  2.9 0.9 %copy-done.3 = f32[1,32,704]{2,1,0:T(8,128)S(1)} copy-done((f32[1,32,704]{2,1,0:T(8,128)S(1)}, f32[1,32,704]{2,1,0:T(8,128)}, u32[]{:S(2)}) %copy-start.3) | copy-done | bytes 90136
  3.7 0.0 copy-start.4
  3.7 0.9 %copy-done.4 = f32[1,32,704]{2,1,0:T(8,128)S(1)} copy-done((f32[1,32,704]{2,1,0:T(8,128)S(1)}, f32[1,32,704]{2,1,0:T(8,128)}, u32[]{:S(2)}) %copy-start.4) | copy-done | bytes 90136
  4.6 0.0 copy-start.5
  4.6 0.9 %copy-done.5 = f32[1,32,704]{2,1,0:T(8,128)S(1)} copy-done((f32[1,32,704]{2,1,0:T(8,128)S(1)}, f32[1,32,704]{2,1,0:T(8,128)}, u32[]{:S(2)}) %copy-start.5) | copy-done | bytes 90136
  5.5 34.1 %shard_map.77 = (f32[1,32,704]{2,1,0:T(8,128)S(1)}, bf16[32,4096]{1,0:T(8,128)(2,1)S(1)}, bf16[32,768]{1,0:T(8,128)(2,1)S(1)}) custom-call(bf16[1,128,4096]{2,1,0:T(8,128)(2,1)S(1)} %copy-done.1, bf16[1,128,1536]{2,1,0:T(8,128)(2,1)S(1)} %copy-done.2, f32[1,32,704]{2,1,0:T(8,128)S(1)} %copy-done.3, f32[1,32,704]{2,1,0:T(8,128)S(1)} %copy-done.4, ...), custom_call_target="tpu_custom_call" | custom-call | tf_op jit(solution)/shard_map/pallas_call | solution.py:236
  39.6 0.0 copy-start
  39.7 2.8 %copy-done = bf16[1,4096,768]{2,1,0:T(8,128)(2,1)S(1)} copy-done((bf16[1,4096,768]{2,1,0:T(8,128)(2,1)S(1)}, bf16[1,4096,768]{2,1,0:T(8,128)(2,1)}, u32[]{:S(2)}) %copy-start) | copy-done | bytes 6291480
  42.4 5.5 %shard_map.78 = bf16[1,4096,768]{2,1,0:T(8,128)(2,1)} custom-call(bf16[1,4096,768]{2,1,0:T(8,128)(2,1)S(1)} %copy-done, bf16[32,4096]{1,0:T(8,128)(2,1)S(1)} %get-tuple-element.5.new_b, bf16[32,768]{1,0:T(8,128)(2,1)S(1)} %get-tuple-element.6.new_a), custom_call_target="tpu_custom_call" | custom-call | tf_op jit(solution)/shard_map/pallas_call | solution.py:271
  47.9 0.6 %copy.9 = f32[1,32,704]{2,1,0:T(8,128)} copy(f32[1,32,704]{2,1,0:T(8,128)S(1)} %get-tuple-element.11) | data formatting | bytes 180224
Async XLA Ops:
  0.6 1.2 %copy-start.1 = (bf16[1,128,4096]{2,1,0:T(8,128)(2,1)S(1)}, bf16[1,128,4096]{2,1,0:T(8,128)(2,1)}, u32[]{:S(2)}) copy-start(bf16[1,128,4096]{2,1,0:T(8,128)(2,1)} %tok.1) | copy-start | bytes 3145732
  1.9 1.0 %copy-start.2 = (bf16[1,128,1536]{2,1,0:T(8,128)(2,1)S(1)}, bf16[1,128,1536]{2,1,0:T(8,128)(2,1)}, u32[]{:S(2)}) copy-start(bf16[1,128,1536]{2,1,0:T(8,128)(2,1)} %cot.1) | copy-start | bytes 1179652
  2.9 0.9 %copy-start.3 = (f32[1,32,704]{2,1,0:T(8,128)S(1)}, f32[1,32,704]{2,1,0:T(8,128)}, u32[]{:S(2)}) copy-start(f32[1,32,704]{2,1,0:T(8,128)} %mas.1) | copy-start | bytes 270340
  3.7 0.9 %copy-start.4 = (f32[1,32,704]{2,1,0:T(8,128)S(1)}, f32[1,32,704]{2,1,0:T(8,128)}, u32[]{:S(2)}) copy-start(f32[1,32,704]{2,1,0:T(8,128)} %mom1.1) | copy-start | bytes 270340
  4.6 0.9 %copy-start.5 = (f32[1,32,704]{2,1,0:T(8,128)S(1)}, f32[1,32,704]{2,1,0:T(8,128)}, u32[]{:S(2)}) copy-start(f32[1,32,704]{2,1,0:T(8,128)} %mom2.1) | copy-start | bytes 270340
  39.6 2.8 %copy-start = (bf16[1,4096,768]{2,1,0:T(8,128)(2,1)S(1)}, bf16[1,4096,768]{2,1,0:T(8,128)(2,1)}, u32[]{:S(2)}) copy-start(bf16[1,4096,768]{2,1,0:T(8,128)(2,1)} %weight.1) | copy-start | bytes 18874372

commit v2 on v1

--- a/solution.py
+++ b/solution.py
@@ -32,8 +32,8 @@
 
 
 def update_kernel(
-    nz, scale, tok, cot, mas, mom1, mom2, ren, out_b, out_a,
-    both, frame, gat, fac, snd_x, rcv_x, own, snd_z, rcv_z, allf,
+    nz, scale, tok, cot, mas_hbm, mom1_hbm, mom2_hbm, weight, ren, out_b, out_a, held,
+    both, mas, mom1, mom2, frame, gat, fac, snd_x, rcv_x, own, snd_z, rcv_z, allf,
     in_sem, g_send, g_recv, x_send, x_recv, z_send, z_recv, f_send, f_recv,
 ):
     width = tok.shape[2]
@@ -52,8 +52,12 @@
 
     in_tok = pltpu.make_async_copy(tok.at[0], both.at[:, pl.ds(0, width)], in_sem.at[0])
     in_cot = pltpu.make_async_copy(cot.at[0], both.at[:, pl.ds(width, hidden_units)], in_sem.at[1])
-    in_tok.start()
-    in_cot.start()
+    in_mas = pltpu.make_async_copy(mas_hbm, mas, in_sem.at[2])
+    in_mom1 = pltpu.make_async_copy(mom1_hbm, mom1, in_sem.at[3])
+    in_mom2 = pltpu.make_async_copy(mom2_hbm, mom2, in_sem.at[4])
+    in_weight = pltpu.make_async_copy(weight, held, in_sem.at[5])
+    for copy in (in_mas, in_tok, in_cot, in_mom1, in_mom2, in_weight):
+        copy.start()
 
     barrier = pltpu.get_barrier_semaphore()
     for d in range(1, nz):
@@ -65,6 +69,7 @@
         frame[:, :block] = ref[0]
         return pltpu.roll(frame[...], x * shift, 1)
 
+    in_mas.wait()
     master = framed(mas)
     gat[x, z] = master.astype(jnp.bfloat16)
     pl.semaphore_wait(barrier, nz)
@@ -166,6 +171,8 @@
         own[row, :, :main] = part
         own[row, :, main:] = last
 
+    in_mom1.wait()
+    in_mom2.wait()
     moment_one = framed(mom1)
     moment_two = framed(mom2)
 
@@ -215,11 +222,22 @@
     out_a[...] = (mine.astype(jnp.float32) * low_rank_scale).astype(jnp.bfloat16)
     for copy in sends:
         copy.wait_send()
-
-
-def merge_kernel(weight, new_b, new_a, merged):
-    product = lax.dot_general(new_b[...], new_a[...], TN, preferred_element_type=jnp.float32)
-    merged[0] = (weight[0].astype(jnp.float32) + product).astype(jnp.bfloat16)
+    in_weight.wait()
+
+
+def merge_kernel(step, weight, new_b, new_a, ren, merged, ren_out, staged, sem):
+    ren_copy = pltpu.make_async_copy(ren, ren_out, sem.at[0])
+    ren_copy.start()
+    copies = []
+    for i in range(staged.shape[0] // step):
+        part = pl.ds(i * step, step)
+        product = lax.dot_general(new_b[:, part], new_a[...], TN, preferred_element_type=jnp.float32)
+        staged[part] = (weight[0, part].astype(jnp.float32) + product).astype(jnp.bfloat16)
+        copy = pltpu.make_async_copy(staged.at[part], merged.at[0, part], sem.at[i + 1])
+        copy.start()
+        copies.append(copy)
+    for copy in copies + [ren_copy]:
+        copy.wait()
 
 
 def fused_shards(nz, tokens, cotangent, frozen_up_weight, master, moment_one, moment_two):
@@ -230,20 +248,24 @@
     lanes = block + 64
     bf16, f32 = jnp.bfloat16, jnp.float32
     vmem = pl.BlockSpec(memory_space=pltpu.VMEM)
-    anywhere = pl.BlockSpec(memory_space=pl.ANY)
+    hbm = pl.BlockSpec(memory_space=pltpu.HBM)
     dma = pltpu.SemaphoreType.DMA
     scale = low_rank_scale / (rows * nz * 2)
-    renewed, new_b, new_a = pl.pallas_call(
+    renewed, new_b, new_a, held = pl.pallas_call(
         functools.partial(update_kernel, nz, scale),
         out_shape=(
-            jax.ShapeDtypeStruct(master.shape, f32),
-            jax.ShapeDtypeStruct((rank, width), bf16),
-            jax.ShapeDtypeStruct((rank, slice_width), bf16),
+            pltpu.VMEM(master.shape, f32),
+            pltpu.VMEM((rank, width), bf16),
+            pltpu.VMEM((rank, slice_width), bf16),
+            pltpu.VMEM(frozen_up_weight.shape, bf16),
         ),
-        in_specs=[anywhere, anywhere, vmem, vmem, vmem],
-        out_specs=(vmem, vmem, vmem),
+        in_specs=[hbm] * 6,
+        out_specs=(vmem,) * 4,
         scratch_shapes=[
             pltpu.VMEM((rows, width + hidden_units), bf16),
+            pltpu.VMEM(master.shape, f32),
+            pltpu.VMEM(master.shape, f32),
+            pltpu.VMEM(master.shape, f32),
             pltpu.VMEM((rank, lanes), f32),
             pltpu.VMEM((2, nz, rank, lanes), bf16),
             pltpu.VMEM((2, nz, rank, lanes), bf16),
@@ -253,7 +275,7 @@
             pltpu.VMEM((nz - 1, rank, lanes), bf16),
             pltpu.VMEM((nz, rank, lanes), bf16),
             pltpu.VMEM((rank, width + hidden_units), bf16),
-            dma((2,)),
+            dma((6,)),
             dma((2 * nz - 1,)),
             dma((2, nz)),
             dma((nz,)),
@@ -264,22 +286,21 @@
             dma((2, nz)),
         ],
         compiler_params=pltpu.CompilerParams(
-            collective_id=0, has_side_effects=True, vmem_limit_bytes=12 * 1024 * 1024
+            collective_id=0, has_side_effects=True, vmem_limit_bytes=56 * 1024 * 1024
         ),
-    )(tokens, cotangent, master, moment_one, moment_two)
+    )(tokens, cotangent, master, moment_one, moment_two, frozen_up_weight)
     step = 512
-    merged = pl.pallas_call(
-        merge_kernel,
-        grid=(width // step,),
-        out_shape=jax.ShapeDtypeStruct(frozen_up_weight.shape, bf16),
-        in_specs=[
-            pl.BlockSpec((1, step, slice_width), lambda i: (0, i, 0)),
-            pl.BlockSpec((rank, step), lambda i: (0, i)),
-            pl.BlockSpec((rank, slice_width), lambda i: (0, 0)),
-        ],
-        out_specs=pl.BlockSpec((1, step, slice_width), lambda i: (0, i, 0)),
-        compiler_params=pltpu.CompilerParams(vmem_limit_bytes=16 * 1024 * 1024),
-    )(frozen_up_weight, new_b, new_a)
+    merged, renewed = pl.pallas_call(
+        functools.partial(merge_kernel, step),
+        out_shape=(
+            jax.ShapeDtypeStruct(frozen_up_weight.shape, bf16),
+            jax.ShapeDtypeStruct(master.shape, f32),
+        ),
+        in_specs=[vmem] * 4,
+        out_specs=(hbm, hbm),
+        scratch_shapes=[pltpu.VMEM((width, slice_width), bf16), dma((width // step + 1,))],
+        compiler_params=pltpu.CompilerParams(vmem_limit_bytes=20 * 1024 * 1024),
+    )(held, new_b, new_a, renewed)
     return merged, renewed
 
 

time: 48.9 us -> 37.5 us (0.77)
  local copies, waits for them, and re-layouts: 8.31 us -> 0 us
  Pallas kernels: 39.6 us -> 36.7 us
    unnamed x13 -> x0, local copies, waits for them, and re-layouts: 8.31 us -> none
    pallas_call x2, Pallas kernels: 39.6 us -> 36.7 us  [the longest x1 33.5 us: fused_shards(): pl.pallas_call(functools.partial(update_kernel, nz, scale), out_shape=(pl...]
where the time goes in v2:
time: 37.5 us; the launch traced here: 37.3 us
  Pallas kernels  36.7 us (98%)
  between operations  0.64 us (2%)
    pallas_call x1, Pallas kernels, fused_shards(): pl.pallas_call(functools.partial(update_kernel, nz, scale), out_shape=(pl...  33.5 us
    pallas_call x1, Pallas kernels, fused_shards(): pl.pallas_call(functools.partial(merge_kernel, step), out_shape=(jax.Shap...  3.21 us

profile of v2, /device:TPU:0, one launch (start us, length us, event | category | flops | bytes accessed | tf_op | source)
XLA Modules:
  0.0 37.3 jit_solution(5493193270894679193)
XLA Ops:
  0.6 33.5 %shard_map.77 = (f32[1,32,704]{2,1,0:T(8,128)S(1)}, bf16[32,4096]{1,0:T(8,128)(2,1)S(1)}, bf16[32,768]{1,0:T(8,128)(2,1)S(1)}, bf16[1,4096,768]{2,1,0:T(8,128)(2,1)S(1)}) custom-call(bf16[1,128,4096]{2,1,0:T(8,128)(2,1)} %tok.1, bf16[1,128,1536]{2,1,0:T(8,128)(2,1)} %cot.1, f32[1,32,704]{2,1,0:T(8,128)} %mas_hbm.1, f32[1,32,704]{2,1,0:T(8,128)} %mom1_hbm.1, ...), custom_call_target="tpu_custom_call" | custom-call | tf_op jit(solution)/shard_map/pallas_call | solution.py:254
  34.1 3.2 %shard_map.78 = (bf16[1,4096,768]{2,1,0:T(8,128)(2,1)}, f32[1,32,704]{2,1,0:T(8,128)}) custom-call(bf16[1,4096,768]{2,1,0:T(8,128)(2,1)S(1)} %get-tuple-element.6.weight, bf16[32,4096]{1,0:T(8,128)(2,1)S(1)} %get-tuple-element.7.new_b, bf16[32,768]{1,0:T(8,128)(2,1)S(1)} %get-tuple-element.8.new_a, f32[1,32,704]{2,1,0:T(8,128)S(1)} %get-tuple-element.9.ren), custom_call_target="tpu_custom_call" | custom-call | tf_op jit(solution)/shard_map/pallas_call | solution.py:293

commit v3 on v2

--- a/solution.py
+++ b/solution.py
@@ -16,6 +16,7 @@
 low_rank_scale = 2.0
 
 MESH = pl.DeviceIdType.MESH
+DIRECT = 1
 NT = (((1,), (1,)), ((), ()))
 TN = (((0,), (0,)), ((), ()))
 
@@ -33,7 +34,7 @@
 
 def update_kernel(
     nz, scale, tok, cot, mas_hbm, mom1_hbm, mom2_hbm, weight, ren, out_b, out_a, held,
-    both, mas, mom1, mom2, frame, gat, fac, snd_x, rcv_x, own, snd_z, rcv_z, allf,
+    both, mas, mom1, mom2, frame, gat, fac, snd_x, rcv_x, own, snd_z, rcv_z, straight, allf,
     in_sem, g_send, g_recv, x_send, x_recv, z_send, z_recv, f_send, f_recv,
 ):
     width = tok.shape[2]
@@ -63,6 +64,8 @@
     for d in range(1, nz):
         pl.semaphore_signal(barrier, inc=1, device_id={"wide": z_at(d)}, device_id_type=MESH)
     pl.semaphore_signal(barrier, inc=1, device_id={"dp": xo}, device_id_type=MESH)
+    for d in (1, nz - 1):
+        pl.semaphore_signal(barrier, inc=1, device_id={"wide": z_at(d), "dp": xo}, device_id_type=MESH)
 
     def framed(ref):
         frame[:, main:] = jnp.zeros((rank, 128), jnp.float32)
@@ -72,17 +75,15 @@
     in_mas.wait()
     master = framed(mas)
     gat[x, z] = master.astype(jnp.bfloat16)
-    pl.semaphore_wait(barrier, nz)
+    pl.semaphore_wait(barrier, nz + 2)
 
     def share(buf, send, recv):
+        targets = [(z_at(d), x) for d in range(2, nz)] + [(z_at(1), x), (z_at(1), xo), (z, xo)]
         sends = []
-        for d in range(1, nz):
+        for i, (row, column) in enumerate(targets):
             sends.append(pltpu.make_async_remote_copy(
-                buf.at[x, z], buf.at[x, z], send.at[d - 1], recv.at[x, z],
-                device_id={"wide": z_at(d)}, device_id_type=MESH))
-        sends.append(pltpu.make_async_remote_copy(
-            buf.at[x, z], buf.at[x, z], send.at[nz - 1], recv.at[x, z],
-            device_id={"dp": xo}, device_id_type=MESH))
+                buf.at[x, z], buf.at[x, z], send.at[i], recv.at[x, z],
+                device_id={"wide": row, "dp": column}, device_id_type=MESH))
         for copy in sends:
             copy.start()
         return sends
@@ -130,16 +131,16 @@
         back = back + jnp.where(b_main, 0.0, part) + jnp.where(b_last, 0.0, last)
         return hidden, back
 
-    for d in range(nz):
-        if d:
-            sends.append(forward(gat, g_send, g_recv, d))
+    hidden, back = project(z, x, hidden, back)
+    for d in range(2, nz):
+        sends.append(forward(gat, g_send, g_recv, d))
         hidden, back = project(z_at(nz - d), x, hidden, back)
+    arrived(gat, g_recv, x, z_at(nz - 1))
+    hidden, back = project(z_at(nz - 1), x, hidden, back)
     for d in range(nz):
         row = z_at(nz - d)
         arrived(gat, g_recv, xo, row)
         hidden, back = project(row, xo, hidden, back)
-    for copy in sends:
-        copy.wait_send()
     hidden = hidden.astype(jnp.bfloat16).astype(jnp.float32)
     back = back.astype(jnp.bfloat16).astype(jnp.float32)
 
@@ -154,22 +155,25 @@
             both[:, pl.ds(pl.multiple_of(begin + main, 128), 128)], preferred_element_type=jnp.float32)
         return part, last
 
+    direct = DIRECT % nz
+    order = [d for d in range(nz - 1, 0, -1) if d != direct] + [direct, 0]
     x_copies = []
-    for i in range(nz):
-        row = z_at(i + 1)
+    for i, d in enumerate(order):
+        row = z_at(d)
+        target = {"wide": row, "dp": xo} if d == direct else {"dp": xo}
         part, last = gradient(row, xo)
-        snd_x[row, :, :main] = part.astype(jnp.bfloat16)
-        snd_x[row, :, main:] = last.astype(jnp.bfloat16)
+        snd_x[i, :, :main] = part.astype(jnp.bfloat16)
+        snd_x[i, :, main:] = last.astype(jnp.bfloat16)
+        landing = straight if d == direct else rcv_x.at[i]
         copy = pltpu.make_async_remote_copy(
-            snd_x.at[row], rcv_x.at[row], x_send.at[i], x_recv.at[row],
-            device_id={"dp": xo}, device_id_type=MESH)
+            snd_x.at[i], landing, x_send.at[i], x_recv.at[i],
+            device_id=target, device_id_type=MESH)
         copy.start()
         x_copies.append(copy)
-    for i in range(nz):
-        row = z_at(i + 1)
-        part, last = gradient(row, x)
-        own[row, :, :main] = part
-        own[row, :, main:] = last
+    for i, d in enumerate(order):
+        part, last = gradient(z_at(d), x)
+        own[i, :, :main] = part
+        own[i, :, main:] = last
 
     in_mom1.wait()
     in_mom2.wait()
@@ -177,17 +181,21 @@
     moment_two = framed(mom2)
 
     z_copies = []
-    for i in range(nz - 1):
-        row = z_at(i + 1)
-        x_copies[i].wait_recv()
-        snd_z[i] = (own[row] + rcv_x[row].astype(jnp.float32)).astype(jnp.bfloat16)
+    for i in (nz - 2, *range(nz - 2)):
+        row = z_at(order[i])
+        part = own[i]
+        if order[i] != direct:
+            x_copies[i].wait_recv()
+            part = part + rcv_x[i].astype(jnp.float32)
+        snd_z[i] = part.astype(jnp.bfloat16)
         copy = pltpu.make_async_remote_copy(
             snd_z.at[i], rcv_z.at[z], z_send.at[i], z_recv.at[z],
             device_id={"wide": row}, device_id_type=MESH)
         copy.start()
         z_copies.append(copy)
     x_copies[nz - 1].wait_recv()
-    total = own[z] + rcv_x[z].astype(jnp.float32)
+    x_copies[nz - 2].wait_recv()
+    total = own[nz - 1] + rcv_x[nz - 1].astype(jnp.float32) + straight[...].astype(jnp.float32)
     for d in range(1, nz):
         row = z_at(nz - d)
         pltpu.make_async_remote_copy(
@@ -200,14 +208,13 @@
     first = x * shift
     valid = (lane >= first) & (lane < first + block)
     fac[x, z] = jnp.where(valid, renewed, 0.0).astype(jnp.bfloat16)
-    sends = share(fac, f_send, f_recv)
+    sends += share(fac, f_send, f_recv)
     frame[...] = pltpu.roll(renewed, lanes - x * shift, 1)
     ren[0] = frame[:, :block]
 
-    for copy in x_copies + z_copies:
-        copy.wait_send()
-    for d in range(1, nz):
+    for d in range(2, nz):
         sends.append(forward(fac, f_send, f_recv, d))
+    arrived(fac, f_recv, x, z_at(nz - 1))
     for d in range(nz):
         arrived(fac, f_recv, xo, z_at(nz - d))
     for row in range(nz):
@@ -220,7 +227,7 @@
     out_b[...] = allf[:, :width]
     mine = allf[:, pl.ds(pl.multiple_of(width + x * slice_width, 128), slice_width)]
     out_a[...] = (mine.astype(jnp.float32) * low_rank_scale).astype(jnp.bfloat16)
-    for copy in sends:
+    for copy in sends + x_copies + z_copies:
         copy.wait_send()
     in_weight.wait()
 
@@ -274,15 +281,16 @@
             pltpu.VMEM((nz, rank, lanes), f32),
             pltpu.VMEM((nz - 1, rank, lanes), bf16),
             pltpu.VMEM((nz, rank, lanes), bf16),
+            pltpu.VMEM((rank, lanes), bf16),
             pltpu.VMEM((rank, width + hidden_units), bf16),
             dma((6,)),
-            dma((2 * nz - 1,)),
+            dma((2 * nz,)),
             dma((2, nz)),
             dma((nz,)),
             dma((nz,)),
             dma((nz - 1,)),
             dma((nz,)),
-            dma((2 * nz - 1,)),
+            dma((2 * nz,)),
             dma((2, nz)),
         ],
         compiler_params=pltpu.CompilerParams(
@@ -337,7 +345,7 @@
 
 
 def frame_fits(nz, nx, width, block, slice_width):
-    if nx != 2 or nz < 2 or nz > 8 or block % 128 != 64 or block < 192 or width % 512 or slice_width % 128:
+    if nx != 2 or nz < 3 or nz > 8 or block % 128 != 64 or block < 192 or width % 512 or slice_width % 128:
         return False
     for row in range(nz):
         for column in range(2):

time: 37.5 us -> 36.3 us (0.968)
  Pallas kernels: 36.7 us -> 35.5 us
    pallas_call x1, Pallas kernels: 33.5 us -> 32.3 us  [fused_shards(): pl.pallas_call(functools.partial(update_kernel, nz, scale), out_shape=(pl...]
where the time goes in v3:
time: 36.3 us; the launch traced here: 36.2 us
  Pallas kernels  35.5 us (98%)
  between operations  0.64 us (2%)
    pallas_call x1, Pallas kernels, fused_shards(): pl.pallas_call(functools.partial(update_kernel, nz, scale), out_shape=(pl...  32.3 us
    pallas_call x1, Pallas kernels, fused_shards(): pl.pallas_call(functools.partial(merge_kernel, step), out_shape=(jax.Shap...  3.2 us

profile of v3, /device:TPU:0, one launch (start us, length us, event | category | flops | bytes accessed | tf_op | source)
XLA Modules:
  0.0 36.2 jit_solution(15573234287097722501)
XLA Ops:
  0.6 32.3 %shard_map.77 = (f32[1,32,704]{2,1,0:T(8,128)S(1)}, bf16[32,4096]{1,0:T(8,128)(2,1)S(1)}, bf16[32,768]{1,0:T(8,128)(2,1)S(1)}, bf16[1,4096,768]{2,1,0:T(8,128)(2,1)S(1)}) custom-call(bf16[1,128,4096]{2,1,0:T(8,128)(2,1)} %tok.1, bf16[1,128,1536]{2,1,0:T(8,128)(2,1)} %cot.1, f32[1,32,704]{2,1,0:T(8,128)} %mas_hbm.1, f32[1,32,704]{2,1,0:T(8,128)} %mom1_hbm.1, ...), custom_call_target="tpu_custom_call" | custom-call | tf_op jit(solution)/shard_map/pallas_call | solution.py:261
  33.0 3.2 %shard_map.78 = (bf16[1,4096,768]{2,1,0:T(8,128)(2,1)}, f32[1,32,704]{2,1,0:T(8,128)}) custom-call(bf16[1,4096,768]{2,1,0:T(8,128)(2,1)S(1)} %get-tuple-element.6.weight, bf16[32,4096]{1,0:T(8,128)(2,1)S(1)} %get-tuple-element.7.new_b, bf16[32,768]{1,0:T(8,128)(2,1)S(1)} %get-tuple-element.8.new_a, f32[1,32,704]{2,1,0:T(8,128)S(1)} %get-tuple-element.9.ren), custom_call_target="tpu_custom_call" | custom-call | tf_op jit(solution)/shard_map/pallas_call | solution.py:301

commit v4 on v3

--- a/solution.py
+++ b/solution.py
@@ -78,7 +78,7 @@
     pl.semaphore_wait(barrier, nz + 2)
 
     def share(buf, send, recv):
-        targets = [(z_at(d), x) for d in range(2, nz)] + [(z_at(1), x), (z_at(1), xo), (z, xo)]
+        targets = [(z_at(d), x) for d in range(2, nz)] + [(z, xo), (z_at(1), xo), (z_at(1), x)]
         sends = []
         for i, (row, column) in enumerate(targets):
             sends.append(pltpu.make_async_remote_copy(
@@ -297,7 +297,7 @@
             collective_id=0, has_side_effects=True, vmem_limit_bytes=56 * 1024 * 1024
         ),
     )(tokens, cotangent, master, moment_one, moment_two, frozen_up_weight)
-    step = 512
+    step = 256
     merged, renewed = pl.pallas_call(
         functools.partial(merge_kernel, step),
         out_shape=(

time: 36.3 us -> 35.5 us (0.978)
  Pallas kernels: 35.5 us -> 34.7 us
    pallas_call x1, Pallas kernels: 32.3 us -> 31.6 us  [fused_shards(): pl.pallas_call(functools.partial(update_kernel, nz, scale), out_shape=(pl...]
where the time goes in v4:
time: 35.5 us; the launch traced here: 35.3 us
  Pallas kernels  34.7 us (98%)
  between operations  0.64 us (2%)
    pallas_call x1, Pallas kernels, fused_shards(): pl.pallas_call(functools.partial(update_kernel, nz, scale), out_shape=(pl...  31.6 us
    pallas_call x1, Pallas kernels, fused_shards(): pl.pallas_call(functools.partial(merge_kernel, step), out_shape=(jax.Shap...  3.11 us

profile of v4, /device:TPU:0, one launch (start us, length us, event | category | flops | bytes accessed | tf_op | source)
XLA Modules:
  0.0 35.3 jit_solution(9031509033578845110)
XLA Ops:
  0.6 31.6 %shard_map.77 = (f32[1,32,704]{2,1,0:T(8,128)S(1)}, bf16[32,4096]{1,0:T(8,128)(2,1)S(1)}, bf16[32,768]{1,0:T(8,128)(2,1)S(1)}, bf16[1,4096,768]{2,1,0:T(8,128)(2,1)S(1)}) custom-call(bf16[1,128,4096]{2,1,0:T(8,128)(2,1)} %tok.1, bf16[1,128,1536]{2,1,0:T(8,128)(2,1)} %cot.1, f32[1,32,704]{2,1,0:T(8,128)} %mas_hbm.1, f32[1,32,704]{2,1,0:T(8,128)} %mom1_hbm.1, ...), custom_call_target="tpu_custom_call" | custom-call | tf_op jit(solution)/shard_map/pallas_call | solution.py:261
  32.2 3.1 %shard_map.78 = (bf16[1,4096,768]{2,1,0:T(8,128)(2,1)}, f32[1,32,704]{2,1,0:T(8,128)}) custom-call(bf16[1,4096,768]{2,1,0:T(8,128)(2,1)S(1)} %get-tuple-element.6.weight, bf16[32,4096]{1,0:T(8,128)(2,1)S(1)} %get-tuple-element.7.new_b, bf16[32,768]{1,0:T(8,128)(2,1)S(1)} %get-tuple-element.8.new_a, f32[1,32,704]{2,1,0:T(8,128)S(1)} %get-tuple-element.9.ren), custom_call_target="tpu_custom_call" | custom-call | tf_op jit(solution)/shard_map/pallas_call | solution.py:301
